TPU v7x, 128 devices: a whole 4x4x4 slice. The times are simulated.
128 devices in a mesh: row: 8 (over x, z_lo), col: 16 (over z_hi, y, core).
Axes of the slice: x: 4, y: 4, z: 4 (z_hi: 2, z_lo: 2; z = z_hi * 2 + z_lo), core: 2. Of those that a mesh axis runs over, the one named last changes fastest.
Arguments:
- object_field: float32 [2, 4096, 8192], P(None, 'row', 'col'), may hold values from -5 to 5
- probe: float32 [2, 256, 256], replicated, may hold values from -6 to 6
- intensity: float32 [1536, 256, 256], P(('row', 'col')), may hold values from 0 to 4
- centers: int32 [1536, 2], P(('row', 'col')), may hold values from 0 to 8191, as said below
- picked: int32 [1536], P(('row', 'col')), may hold values 0 or 1
Outputs:
- object_out: float32 [2, 4096, 8192], P(None, 'row', 'col')
- probe_out: float32 [2, 256, 256], replicated
Inputs may be any that keep to these rules, and one draw needn't show every extreme that they name: `centers`: the frames f with k * 12 <= f < (k + 1) * 12 belong to subdomain k = 16 i + j: their centres lie in rows i * 512 to (i + 1) * 512 - 1 and columns j * 512 to (j + 1) * 512 - 1. Of one subdomain's frames at most 6 have centres in any one quarter of it (upper or lower 512/2 rows times left or right 512/2 columns), and in every subdomain some quarter holds exactly 6.
All inputs are finite; a program needn't handle non-finite values. No bound on the sum of `picked` on one device may be relied on, other than what follows from the above.
Results may differ from a plain program's by a relative error of at most 0.012.
The roundings to bfloat16 on the way count: a program that leaves them out, or rounds other values in their place, can miss the bound.
Values sent between devices are 32-bit elements; how exact they have to be, the bound alone decides.
No kernel may reach another device: no remote copies, remote signals or barrier semaphores. Data moves between devices by JAX's collectives and lax.ppermute only.
A program may use at most 128 MiB of HBM per device.

v0:
```python
import math

import jax
import jax.numpy as jnp
import numpy as np
from jax import lax
from jax.experimental import pallas as pl
from jax.experimental.pallas import tpu as pltpu
from jax.sharding import PartitionSpec as P

ITERS = 2


object_rate = 0.02
probe_gain = 4.0
LANES = 128
SUBLANES = 8
GROUP = 4


def tables(frame_side):
    indices = np.arange(frame_side)
    angle = (indices[:, None] * indices[None, :] % frame_side) * (2.0 * math.pi / frame_side)
    scale = 1.0 / math.sqrt(frame_side)
    real_part = (np.cos(angle) * scale).astype(np.float32).astype(jnp.bfloat16)
    imag_part = (-np.sin(angle) * scale).astype(np.float32).astype(jnp.bfloat16)
    right_mat = np.block([[real_part, imag_part], [-imag_part, real_part]])
    left_mat = np.block([[real_part, -imag_part], [imag_part, real_part]])
    return (jnp.asarray(right_mat), jnp.asarray(left_mat))


def frames_kernel(places, cuts, final, side, info, *refs):
    count, out_count = len(places), len(cuts)
    pieces = refs[:count]
    probe_far, intens, right_far, left_far = refs[count : count + 4]
    outs = refs[count + 4 : count + 4 + out_count]
    probe_grad, region, grad, held, levels, probe, right_mat, left_mat, chosen, in_sems, level_sems, out_sems = refs[
        count + 4 + out_count :
    ]
    arriving = []
    for piece, parts in zip(pieces, places):
        for (row_from, col_from), (row_at, col_at), (rows, cols) in parts:
            arriving.append(
                pltpu.make_async_copy(
                    piece.at[:, row_from : row_from + rows, col_from : col_from + cols],
                    region.at[:, row_at : row_at + rows, col_at : col_at + cols],
                    in_sems.at[len(arriving)],
                )
            )
    for source, target in ((probe_far, probe), (right_far, right_mat), (left_far, left_mat)):
        arriving.append(pltpu.make_async_copy(source, target, in_sems.at[len(arriving)]))
    for copy in arriving:
        copy.start()

    def level_copy(slot):
        return pltpu.make_async_copy(intens.at[slot], levels.at[slot], level_sems.at[slot])

    def pick(slot, found):
        @pl.when(info[slot, 2] != 0)
        def _():
            chosen[found] = slot
            level_copy(slot).start()

        return found + jnp.where(info[slot, 2] != 0, 1, 0)

    total = lax.fori_loop(0, info.shape[0], pick, jnp.int32(0))
    grad[...] = jnp.zeros_like(grad)
    probe_grad[...] = jnp.zeros_like(probe_grad)
    for copy in arriving:
        copy.wait()
    lane = lax.broadcasted_iota(jnp.int32, (side + SUBLANES, LANES), 1)
    line = lax.broadcasted_iota(jnp.int32, (1, SUBLANES, LANES), 1)

    tiles = side // SUBLANES

    def one_group(turns):
        slots = [chosen[jnp.minimum(turn, total - 1)] for turn in turns]
        shares = [jnp.where(turn < total, 1.0, 0.0) for turn in turns]
        places_of = []
        for slot in slots:
            row_at = info[slot, 0]
            col_at = info[slot, 1]
            col_base = pl.multiple_of(col_at // LANES * LANES, LANES)
            row_base = pl.multiple_of(row_at // SUBLANES * SUBLANES, SUBLANES)
            col_shift = col_at - col_base
            row_shift = row_at - row_base
            places_of.append((row_base, col_base, row_shift, col_shift))

        def window(lot, part):
            row_base, col_base, row_shift, col_shift = places_of[lot]
            col_back = jnp.where(col_shift == 0, 0, LANES - col_shift)
            row_back = jnp.where(row_shift == 0, 0, SUBLANES - row_shift)
            inside = lane < LANES - col_shift
            inside_row = line < SUBLANES - row_shift
            rows = pl.ds(row_base, side + SUBLANES)
            turned = [
                pltpu.roll(region[part, rows, pl.ds(pl.multiple_of(col_base + LANES * k, LANES), LANES)], col_back, 1)
                for k in range(3)
            ]
            for k in range(2):
                piece = jnp.where(inside, turned[k], turned[k + 1]).reshape(tiles + 1, SUBLANES, LANES)
                piece = pltpu.roll(piece, row_back, 1)
                piece = jnp.where(inside_row, piece[:tiles], piece[1:]).reshape(side, LANES)
                held[lot, part, :, k * LANES : (k + 1) * LANES] = piece

        def spread(lot, part, value):
            row_base, col_base, row_shift, col_shift = places_of[lot]
            outside = lane >= col_shift
            outside_row = line >= row_shift
            rows = pl.ds(row_base, side + SUBLANES)
            nothing = jnp.zeros((1, SUBLANES, LANES), jnp.float32)
            turned = []
            for k in range(2):
                piece = value[:, k * LANES : (k + 1) * LANES].reshape(tiles, SUBLANES, LANES)
                piece = pltpu.roll(piece, row_shift, 1)
                piece = jnp.where(
                    outside_row,
                    jnp.concatenate([piece, nothing], axis=0),
                    jnp.concatenate([nothing, piece], axis=0),
                ).reshape(side + SUBLANES, LANES)
                turned.append(pltpu.roll(piece, col_shift, 1))
            first, second = turned
            grad[part, rows, pl.ds(col_base, LANES)] += jnp.where(outside, first, 0.0)
            grad[part, rows, pl.ds(pl.multiple_of(col_base + LANES, LANES), LANES)] += jnp.where(outside, second, first)
            grad[part, rows, pl.ds(pl.multiple_of(col_base + 2 * LANES, LANES), LANES)] += jnp.where(outside, 0.0, second)

        lots = range(len(slots))

        def exit_wave(lot):
            window(lot, 0)
            window(lot, 1)
            win_re, win_im = held[lot, 0], held[lot, 1]
            pr_re, pr_im = probe[0], probe[1]
            exit_re = pr_re * win_re - pr_im * win_im
            exit_im = pr_re * win_im + pr_im * win_re
            return jnp.concatenate([exit_re, exit_im], axis=1).astype(jnp.bfloat16)

        def to_wave(flat):
            wave = jnp.dot(flat, right_mat[...], preferred_element_type=jnp.float32).astype(jnp.bfloat16)
            return jnp.concatenate([wave[:, :side], wave[:, side:]], axis=0)

        def to_far(stacked):
            return jnp.dot(left_mat[...], stacked, preferred_element_type=jnp.float32)

        def to_weighted(far, lot):
            far_re, far_im = far[:side], far[side:]
            mismatch = (far_re * far_re + far_im * far_im - levels[slots[lot]]) * shares[lot]
            return jnp.concatenate([mismatch * far_re, mismatch * far_im], axis=0).astype(jnp.bfloat16)

        def to_returned(weighted):
            returned = jnp.dot(right_mat[...], weighted, preferred_element_type=jnp.float32).astype(jnp.bfloat16)
            return jnp.concatenate([returned[:side], returned[side:]], axis=1)

        def to_gradient(flat_back):
            return jnp.dot(flat_back, left_mat[...], preferred_element_type=jnp.float32)

        def add(lot, gradient):
            pr_re, pr_im = probe[0], probe[1]
            gr_re, gr_im = gradient[:, :side], gradient[:, side:]
            win_re, win_im = held[lot, 0], held[lot, 1]
            probe_grad[0] += win_re * gr_re + win_im * gr_im
            probe_grad[1] += win_re * gr_im - win_im * gr_re
            spread(lot, 0, pr_re * gr_re + pr_im * gr_im)
            spread(lot, 1, pr_re * gr_im - pr_im * gr_re)

        for turn, slot in zip(turns, slots):

            @pl.when(turn < total)
            def _(slot=slot):
                level_copy(slot).wait()

        waves = [to_wave(exit_wave(lot)) for lot in lots]
        fars = [to_far(wave) for wave in waves]
        weights = [to_weighted(fars[lot], lot) for lot in lots]
        returns = [to_returned(weighted) for weighted in weights]
        grads = [to_gradient(returned) for returned in returns]
        for lot in lots:
            add(lot, grads[lot])

    def one_step(at, carried):
        one_group([GROUP * at + lot for lot in range(GROUP)])
        return carried

    lax.fori_loop(0, (total + GROUP - 1) // GROUP, one_step, 0)
    full = region.shape[1]
    width = side // 2
    if final:
        own = slice(width, full - width)
        for rows, cols in ((slice(0, width), slice(0, full)), (slice(full - width, full), slice(0, full)),
                           (own, slice(0, width)), (own, slice(full - width, full))):
            grad[:, rows, cols] = -object_rate * grad[:, rows, cols]
        grad[:, own, own] = region[:, own, own] - object_rate * grad[:, own, own]
    leaving = []
    for out, parts in zip(outs, cuts):
        for (row_from, col_from), (row_at, col_at), (rows, cols) in parts:
            leaving.append(
                pltpu.make_async_copy(
                    grad.at[:, row_from : row_from + rows, col_from : col_from + cols],
                    out.at[:, row_at : row_at + rows, col_at : col_at + cols],
                    out_sems.at[len(leaving)],
                )
            )
    for copy in leaving:
        copy.start()
    for copy in leaving:
        copy.wait()


def frames(info, placed, probe, intensity, mats, full, cuts, final):
    side = probe.shape[-1]
    vmem = pl.BlockSpec(memory_space=pltpu.VMEM)
    smem = pl.BlockSpec(memory_space=pltpu.SMEM)
    anywhere = pl.BlockSpec(memory_space=pl.ANY)
    far = pl.BlockSpec(memory_space=pltpu.HBM)
    pieces = [piece for piece, parts in placed]
    places = [parts for piece, parts in placed]
    out_shapes = []
    for parts in cuts:
        rows = max(row_at + rows for _, (row_at, _), (rows, _) in parts)
        cols = max(col_at + cols for _, (_, col_at), (_, cols) in parts)
        out_shapes.append(jax.ShapeDtypeStruct((2, rows, cols), jnp.float32))
    out_shapes.append(jax.ShapeDtypeStruct(probe.shape, jnp.float32))

    def kernel(*refs):
        frames_kernel(places, cuts, final, side, *refs)

    return pl.pallas_call(
        kernel,
        out_shape=out_shapes,
        in_specs=[smem] + [anywhere] * len(pieces) + [far] * 4,
        out_specs=[far] * len(cuts) + [vmem],
        scratch_shapes=[
            pltpu.VMEM((2, full, full), jnp.float32),
            pltpu.VMEM((2, full, full), jnp.float32),
            pltpu.VMEM((GROUP, *probe.shape), jnp.float32),
            pltpu.VMEM(intensity.shape, jnp.float32),
            pltpu.VMEM(probe.shape, jnp.float32),
            pltpu.VMEM(mats[0].shape, mats[0].dtype),
            pltpu.VMEM(mats[1].shape, mats[1].dtype),
            pltpu.SMEM((info.shape[0],), jnp.int32),
            pltpu.SemaphoreType.DMA((sum(len(parts) for parts in places) + 3,)),
            pltpu.SemaphoreType.DMA((info.shape[0],)),
            pltpu.SemaphoreType.DMA((sum(len(parts) for parts in cuts),)),
        ],
        compiler_params=pltpu.CompilerParams(vmem_limit_bytes=(40 if final else 60) * 1024 * 1024),
        name="frames",
    )(info, *pieces, probe, intensity, *mats)


def shifted(array, axis, by):
    count = lax.axis_size(axis)
    return lax.ppermute(array, axis, [(i, (i + by) % count) for i in range(count)])


def moved(array, axis, by):
    row_count, col_count = lax.axis_size("row"), lax.axis_size("col")
    sizes = {"x": row_count // 2, "z": 4, "y": col_count // 4, "core": 2}
    pairs = []
    for x in range(sizes["x"]):
        for z in range(sizes["z"]):
            for y in range(sizes["y"]):
                for core in range(sizes["core"]):
                    ends = []
                    for step in (0, by):
                        at = {"x": x, "z": z, "y": y, "core": core}
                        at[axis] = (at[axis] + step) % sizes[axis]
                        row = at["x"] * 2 + at["z"] % 2
                        col = (at["z"] // 2) * (col_count // 2) + at["y"] * 2 + at["core"]
                        ends.append(row * col_count + col)
                    pairs.append(tuple(ends))
    return lax.ppermute(array, ("row", "col"), pairs)


def core_and_y():
    col = lax.axis_index("col")
    return (col % 2, col // 2 % (lax.axis_size("col") // 4), lax.axis_size("col") // 4)


def core_share(part):
    core, _, _ = core_and_y()
    halves = part.reshape(2, -1, part.shape[-1])
    mine = lax.dynamic_index_in_dim(halves, core, 0, False)
    other = lax.dynamic_index_in_dim(halves, 1 - core, 0, False)
    return mine + moved(other, "core", 1)


def y_share(half):
    _, y, y_count = core_and_y()
    quarters = half.reshape(y_count, -1, half.shape[-1])
    total = lax.dynamic_index_in_dim(quarters, y, 0, False)
    arrived = [
        moved(lax.dynamic_index_in_dim(quarters, (y + by) % y_count, 0, False), "y", by) for by in range(1, y_count)
    ]
    for value in arrived:
        total = total + value
    return total


def sum_along(total, axis, count):
    for value in [moved(total, axis, by) for by in range(1, count)]:
        total = total + value
    return total


def y_gathered(total):
    _, y, y_count = core_and_y()
    gathered = [total] + [moved(total, "y", by) for by in range(1, y_count)]
    half = jnp.zeros((y_count, *total.shape), jnp.float32)
    for by, value in enumerate(gathered):
        half = lax.dynamic_update_index_in_dim(half, value, (y - by) % y_count, 0)
    return half


def both_halves(half, shape):
    core, _, _ = core_and_y()
    other = moved(half, "core", 1)
    first = jnp.where(core == 0, half, other)
    second = jnp.where(core == 0, other, half)
    return jnp.concatenate([first, second], axis=0).reshape(shape)


def on_device(object_field, probe, intensity, centers, picked):
    tile = object_field.shape[1]
    side = probe.shape[-1]
    width = side // 2
    half = tile // 2
    full = tile + side
    rows_all = tile * lax.axis_size("row")
    cols_all = tile * lax.axis_size("col")
    frames_total = intensity.shape[0] * lax.axis_size("row") * lax.axis_size("col")
    mats = tables(side)
    local_row = (centers[:, 0] - lax.axis_index("row") * tile) % rows_all
    local_col = (centers[:, 1] - lax.axis_index("col") * tile) % cols_all
    info = jnp.stack([local_row, local_col, picked], axis=1)
    low, high, last = width, tile - width, full - width

    def whole(row, col, rows, cols):
        return [((0, 0), (row, col), (rows, cols))]

    def cut(row, col, rows, cols):
        return [((row, col), (0, 0), (rows, cols))]

    def outer(rows):
        return jnp.concatenate([rows[:, :, :width], rows[:, :, high:]], axis=2)

    below_outer = shifted(outer(object_field[:, :width]), "row", -1)
    above_outer = shifted(outer(object_field[:, high:]), "row", 1)
    below_inner = shifted(object_field[:, :width, low:high], "row", -1)
    above_inner = shifted(object_field[:, high:, low:high], "row", 1)
    at_left = shifted(object_field[:, :, high:], "col", 1)
    at_right = shifted(object_field[:, :, :width], "col", -1)
    ends_left = shifted(jnp.concatenate([above_outer[:, :, width:], below_outer[:, :, width:]], axis=1), "col", 1)
    corners = jnp.concatenate([above_outer[:, :, :width], below_outer[:, :, :width]], axis=1)
    corners, above_inner, below_inner, ends_left = lax.optimization_barrier(
        (corners, above_inner, below_inner, ends_left)
    )
    ends_right = shifted(corners, "col", -1)

    def two_columns(row):
        return [((0, 0), (row, width), (width, width)), ((0, width), (row, tile), (width, width))]

    placed = [
        (above_outer, two_columns(0)),
        (above_inner, whole(0, side, width, side)),
        (object_field, whole(width, width, tile, tile)),
        (below_outer, two_columns(last)),
        (below_inner, whole(last, side, width, side)),
        (at_left, whole(width, 0, tile, width)),
        (at_right, whole(width, last, tile, width)),
        (ends_left, [((0, 0), (0, 0), (width, width)), ((width, 0), (last, 0), (width, width))]),
        (ends_right, [((0, 0), (0, last), (width, width)), ((width, 0), (last, last), (width, width))]),
    ]
    both_edges = [((0, width), (0, 0), (full, width)), ((0, tile), (0, width), (full, width))]
    cuts = [
        cut(0, 0, full, width),
        cut(0, last, full, width),
        cut(0, side, side, side),
        cut(tile, side, side, side),
        cut(side, side, side, side),
        both_edges,
    ]
    grad_left, grad_right, inner_top, inner_low, inner_mid, edges, probe_part = frames(
        info, placed, probe, intensity, mats, full, cuts, False
    )

    x_count = lax.axis_size("row") // 2
    inner_up = shifted(inner_top, "row", -1)
    inner_down = shifted(inner_low, "row", 1)
    from_right = shifted(grad_left, "col", -1)
    from_left = shifted(grad_right, "col", 1)
    share = core_share(probe_part)
    share, from_right, from_left, edges, inner_top, inner_low, inner_mid = lax.optimization_barrier(
        (share, from_right, from_left, edges, inner_top, inner_low, inner_mid)
    )
    edges = edges + jnp.concatenate([from_left, from_right], axis=2)
    edges_up = shifted(edges[:, :side], "row", -1)
    edges_down = shifted(edges[:, tile:], "row", 1)
    share = y_share(share)
    share, inner_up, inner_down = lax.optimization_barrier((share, inner_up, inner_down))
    half_sum = y_gathered(sum_along(sum_along(share, "x", x_count), "z", 4))
    old_edges = jnp.concatenate([above_outer, outer(object_field), below_outer], axis=1)
    new_edges = jnp.concatenate(
        [
            old_edges[:, :side] - object_rate * (edges[:, :side] + edges_down),
            old_edges[:, side:tile] - object_rate * edges[:, side:tile],
            old_edges[:, tile:] - object_rate * (edges[:, tile:] + edges_up),
        ],
        axis=1,
    )
    left = shifted(new_edges[:, :, width:], "col", 1)
    right = shifted(new_edges[:, :, :width], "col", -1)
    half_sum, left, right = lax.optimization_barrier((half_sum, left, right))
    probe_total = both_halves(half_sum, probe.shape)
    old_inner = jnp.concatenate([above_inner, object_field[:, :, low:high], below_inner], axis=1)
    new_inner = jnp.concatenate(
        [
            old_inner[:, :side] - object_rate * (inner_top + inner_down),
            old_inner[:, side:tile] - object_rate * inner_mid,
            old_inner[:, tile:] - object_rate * (inner_low + inner_up),
        ],
        axis=1,
    )
    probe_now = probe - probe_gain / frames_total * probe_total

    placed = [
        (left, whole(0, 0, full, width)),
        (right, whole(0, last, full, width)),
        (new_edges, [((0, 0), (0, width), (full, width)), ((0, width), (0, tile), (full, width))]),
        (new_inner, whole(0, side, full, side)),
    ]
    reach = width + half
    cuts = [
        cut(0, 0, reach, reach),
        cut(reach, 0, full - reach, reach),
        cut(0, reach, reach, width),
        cut(0, tile, reach, 2 * width),
        cut(reach, reach, full - reach, full - reach),
    ]
    out_top, out_rest, here_0, here_1, here_rest, probe_part = frames(
        info, placed, probe_now, intensity, mats, full, cuts, True
    )

    up_0 = shifted(here_0, "row", -1)
    got_top = shifted(out_top, "col", -1)
    share = core_share(probe_part)
    share, got_top, up_0 = lax.optimization_barrier((share, got_top, up_0))
    up_1 = shifted(here_1[:, :, :width] + got_top[:, :, :width], "row", -1)
    up_2 = shifted(here_1[:, :, width:] + got_top[:, :, width : 2 * width], "row", -1)
    up_3 = shifted(got_top[:, :, 2 * width :], "row", -1)
    share = y_share(share)
    share, out_rest, up_1 = lax.optimization_barrier((share, out_rest, up_1))
    got_rest = shifted(out_rest, "col", -1)
    share = sum_along(share, "x", x_count)
    share, up_2, got_rest = lax.optimization_barrier((share, up_2, got_rest))
    half_sum = y_gathered(sum_along(share, "z", 4))
    half_sum, up_3 = lax.optimization_barrier((half_sum, up_3))
    probe_total = both_halves(half_sum, probe.shape)
    mine = jnp.concatenate(
        [
            here_rest[:, :, :width],
            here_rest[:, :, width : 2 * width] + got_rest[:, :, :width],
            here_rest[:, :, 2 * width :] + got_rest[:, :, width : 2 * width],
            got_rest[:, :, 2 * width :],
        ],
        axis=2,
    )
    got = jnp.concatenate([up_0, up_1, up_2, up_3], axis=2)
    moved = jnp.concatenate(
        [mine[:, :width], mine[:, width:] + got[:, : 2 * width], got[:, 2 * width :]], axis=1
    )
    return (moved, probe_now - probe_gain / frames_total * probe_total)


def solution(mesh):
    in_specs = (
        P(None, "row", "col"),
        P(),
        P(("row", "col"), None, None),
        P(("row", "col"), None),
        P(("row", "col")),
    )
    out_specs = (P(None, "row", "col"), P())
    return jax.shard_map(
        on_device, mesh=mesh, in_specs=in_specs, out_specs=out_specs, check_vma=False
    )
```

profile of v0, /device:TPU:1, one launch (start us, length us, event | category | flops | bytes accessed | tf_op | source)
XLA Modules:
  0.0 247.5 jit_solution(8515632682859976788)
XLA Ops:
  2.0 4.7 %collective-permute-start.1 = (f32[2,128,256]{2,1,0:T(8,128)S(1)}, f32[2,128,256]{2,1,0:T(8,128)S(1)}, u32[]{:S(2)}, u32[]{:S(2)}) collective-permute-start(f32[2,128,256]{2,1,0:T(8,128)S(1)} %pad_maximum_fusion.13), channel_id=1, source_target_pairs={{0,112},{16,0},{32,16},{48,32},{64,48},{80,64},{96,80},{112,96},{1... | collective-permute-start | bytes 786440 | tf_op jit(solution)/shard_map/ppermute | solution.py:252
  7.8 3.4 %collective-permute-start.3 = (f32[2,128,256]{2,1,0:T(8,128)}, f32[2,128,256]{2,1,0:T(8,128)}, u32[]{:S(2)}, u32[]{:S(2)}) collective-permute-start(f32[2,128,256]{2,1,0:T(8,128)} %get-tuple-element.95), channel_id=1, source_target_pairs={{0,112},{16,0},{32,16},{48,32},{64,48},{80,64},{96,80},{112,96},{1... | collective-permute-start | bytes 786440 | tf_op jit(solution)/shard_map/ppermute | solution.py:252
  11.7 10.9 %collective-permute-done.refs_1_ = f32[2,128,256]{2,1,0:T(8,128)S(1)} collective-permute-done((f32[2,128,256]{2,1,0:T(8,128)S(1)}, f32[2,128,256]{2,1,0:T(8,128)S(1)}, u32[]{:S(2)}, u32[]{:S(2)}) %collective-permute-start) | collective-permute-done | bytes 262176 | tf_op jit(solution)/shard_map/ppermute | solution.py:252
  24.1 2.2 collective-permute-start.4
  30.0 5.0 %collective-permute-start.7 = (f32[2,256,128]{2,1,0:T(8,128)}, f32[2,256,128]{2,1,0:T(8,128)}, u32[]{:S(2)}, u32[]{:S(2)}) collective-permute-start(f32[2,256,128]{2,1,0:T(8,128)} %pad_maximum_fusion.14), channel_id=1, source_target_pairs={{0,15},{1,0},{2,1},{3,2},{4,3},{5,4},{6,5},{7,6},{8,7},{9,8},{10,9... | collective-permute-start | bytes 786440 | tf_op jit(solution)/shard_map/ppermute | solution.py:252
  36.2 2.8 %collective-permute-done.7.refs_9_ = f32[2,256,128]{2,1,0:T(8,128)} collective-permute-done((f32[2,256,128]{2,1,0:T(8,128)}, f32[2,256,128]{2,1,0:T(8,128)}, u32[]{:S(2)}, u32[]{:S(2)}) %collective-permute-start.7) | collective-permute-done | bytes 262176 | tf_op jit(solution)/shard_map/ppermute | solution.py:252
  39.0 19.2 %frames.2 = (f32[2,768,128]{2,1,0:T(8,128)}, f32[2,768,128]{2,1,0:T(8,128)}, f32[2,256,256]{2,1,0:T(8,128)}, f32[2,256,256]{2,1,0:T(8,128)}, f32[2,256,256]{2,1,...) custom-call(s32[12,3]{1,0:T(8,128)} %copy.13.refs_0_, f32[2,128,256]{2,1,0:T(8,128)} %copy-done.6, ...), custom_call_target="tpu_custom_call" | custom-call | tf_op jit(solution)/shard_map/frames/pallas_call | solution.py:227
  59.7 7.2 %collective-permute-start.8 = (f32[256,256]{1,0:T(8,128)S(1)}, f32[256,256]{1,0:T(8,128)S(1)}, u32[]{:S(2)}, u32[]{:S(2)}) collective-permute-start(f32[256,256]{1,0:T(8,128)S(1)} %dynamic-slice_bitcast_fusion.1), channel_id=1, source_target_pairs={{0,1},{1,0},{2,3},{3,2},{4,5},{5,4},{6,7},{7,6},{16,17},{17,16},{1... | collective-permute-start | bytes 786440 | tf_op jit(solution)/shard_map/ppermute | solution.py:271
  66.9 4.5 %collective-permute-start.14 = (f32[2,256,256]{2,1,0:T(8,128)}, f32[2,256,256]{2,1,0:T(8,128)S(1)}, u32[]{:S(2)}, u32[]{:S(2)}) collective-permute-start(f32[2,256,256]{2,1,0:T(8,128)} %get-tuple-element.61), channel_id=1, source_target_pairs={{0,112},{16,0},{32,16},{48,32},{64,48},{80,64},{96,80},{112,96},{1... | collective-permute-start | bytes 1572872 | tf_op jit(solution)/shard_map/ppermute | solution.py:252
  72.8 11.2 %collective-permute-start.12 = (f32[64,256]{1,0:T(8,128)S(1)}, f32[64,256]{1,0:T(8,128)S(1)}, u32[]{:S(2)}, u32[]{:S(2)}) collective-permute-start(f32[64,256]{1,0:T(8,128)S(1)} %get-tuple-element.121), channel_id=1, source_target_pairs={{0,4},{1,5},{2,6},{3,7},{4,0},{5,1},{6,2},{7,3},{16,20},{17,21},{1... | collective-permute-start | bytes 196616 | tf_op jit(solution)/shard_map/ppermute | solution.py:271
  84.0 2.0 maximum_add_fusion
  87.1 7.6 %collective-permute-start.25 = (f32[2,256,256]{2,1,0:T(8,128)S(1)}, f32[2,256,256]{2,1,0:T(8,128)S(1)}, u32[]{:S(2)}, u32[]{:S(2)}) collective-permute-start(f32[2,256,256]{2,1,0:T(8,128)S(1)} %get-tuple-element.105), channel_id=1, source_target_pairs={{0,16},{16,32},{32,48},{48,64},{64,80},{80,96},{96,112},{112,0},{1... | collective-permute-start | bytes 1572872 | tf_op jit(solution)/shard_map/ppermute | solution.py:252
  94.9 16.5 %collective-permute-done.14 = f32[2,256,256]{2,1,0:T(8,128)S(1)} collective-permute-done((f32[2,256,256]{2,1,0:T(8,128)}, f32[2,256,256]{2,1,0:T(8,128)S(1)}, u32[]{:S(2)}, u32[]{:S(2)}) %collective-permute-start.14) | collective-permute-done | bytes 524320 | tf_op jit(solution)/shard_map/ppermute | solution.py:252
  113.2 2.1 collective-permute-start.18
  126.9 4.6 %collective-permute-start.23 = (f32[64,256]{1,0:T(8,128)S(1)}, f32[64,256]{1,0:T(8,128)S(1)}, u32[]{:S(2)}, u32[]{:S(2)}) collective-permute-start(f32[64,256]{1,0:T(8,128)S(1)} %get-tuple-element.87), channel_id=1, source_target_pairs={{0,4},{1,5},{2,6},{3,7},{4,0},{5,1},{6,2},{7,3},{16,20},{17,21},{1... | collective-permute-start | bytes 196616 | tf_op jit(solution)/shard_map/ppermute | solution.py:271
  132.6 9.6 %collective-permute-done.22 = f32[64,256]{1,0:T(8,128)S(1)} collective-permute-done((f32[64,256]{1,0:T(8,128)S(1)}, f32[64,256]{1,0:T(8,128)S(1)}, u32[]{:S(2)}, u32[]{:S(2)}) %collective-permute-start.22) | collective-permute-done | bytes 65568 | tf_op jit(solution)/shard_map/ppermute | solution.py:271
  147.4 15.7 %frames.3 = (f32[2,384,384]{2,1,0:T(8,128)S(1)}, f32[2,384,384]{2,1,0:T(8,128)S(1)}, f32[2,384,128]{2,1,0:T(8,128)S(1)}, f32[2,384,256]{2,1,0:T(8,128)S(1)}, f32...) custom-call(s32[12,3]{1,0:T(8,128)S(1)} %copy-done.2, f32[2,768,128]{2,1,0:T(8,128)} %collective-permute-done.27.refs_1_, ...), custom_call_target="tpu_custom_call" | custom-call | tf_op jit(solution)/shard_map/frames/pallas_call | solution.py:227
  163.2 5.2 %collective-permute-start.30 = (f32[256,256]{1,0:T(8,128)S(1)}, f32[256,256]{1,0:T(8,128)S(1)}, u32[]{:S(2)}, u32[]{:S(2)}) collective-permute-start(f32[256,256]{1,0:T(8,128)S(1)} %dynamic-slice_bitcast_fusion), channel_id=1, source_target_pairs={{0,1},{1,0},{2,3},{3,2},{4,5},{5,4},{6,7},{7,6},{16,17},{17,16},{1... | collective-permute-start | bytes 786440 | tf_op jit(solution)/shard_map/ppermute | solution.py:271
  170.3 8.8 %collective-permute-done.32 = f32[2,384,128]{2,1,0:T(8,128)S(1)} collective-permute-done((f32[2,384,128]{2,1,0:T(8,128)S(1)}, f32[2,384,128]{2,1,0:T(8,128)S(1)}, u32[]{:S(2)}, u32[]{:S(2)}) %collective-permute-start.32) | collective-permute-done | bytes 393248 | tf_op jit(solution)/shard_map/ppermute | solution.py:252
  179.3 4.0 %collective-permute-start.36 = (f32[2,384,128]{2,1,0:T(8,128)S(1)}, f32[2,384,128]{2,1,0:T(8,128)S(1)}, u32[]{:S(2)}, u32[]{:S(2)}) collective-permute-start(f32[2,384,128]{2,1,0:T(8,128)S(1)} %get-tuple-element.102), channel_id=1, source_target_pairs={{0,112},{16,0},{32,16},{48,32},{64,48},{80,64},{96,80},{112,96},{1... | collective-permute-start | bytes 1179656 | tf_op jit(solution)/shard_map/ppermute | solution.py:252
  183.5 9.6 %collective-permute-start.34 = (f32[64,256]{1,0:T(8,128)S(1)}, f32[64,256]{1,0:T(8,128)S(1)}, u32[]{:S(2)}, u32[]{:S(2)}) collective-permute-start(f32[64,256]{1,0:T(8,128)S(1)} %get-tuple-element.118), channel_id=1, source_target_pairs={{0,4},{1,5},{2,6},{3,7},{4,0},{5,1},{6,2},{7,3},{16,20},{17,21},{1... | collective-permute-start | bytes 196616 | tf_op jit(solution)/shard_map/ppermute | solution.py:271
  193.6 2.0 collective-permute-done.34
  197.3 2.4 collective-permute-start.41
  199.6 2.7 %collective-permute-start.40 = (f32[2,384,128]{2,1,0:T(8,128)S(1)}, f32[2,384,128]{2,1,0:T(8,128)S(1)}, u32[]{:S(2)}, u32[]{:S(2)}) collective-permute-start(f32[2,384,128]{2,1,0:T(8,128)S(1)} %get-tuple-element.101), channel_id=1, source_target_pairs={{0,112},{16,0},{32,16},{48,32},{64,48},{80,64},{96,80},{112,96},{1... | collective-permute-start | bytes 1179656 | tf_op jit(solution)/shard_map/ppermute | solution.py:252
  202.6 2.6 %collective-permute-start.39 = (f32[64,256]{1,0:T(8,128)S(1)}, f32[64,256]{1,0:T(8,128)S(1)}, u32[]{:S(2)}, u32[]{:S(2)}) collective-permute-start(f32[64,256]{1,0:T(8,128)S(1)} %fusion.8), channel_id=1, source_target_pairs={{0,96},{1,97},{2,98},{3,99},{4,100},{5,101},{6,102},{7,103},{16,11... | collective-permute-start | bytes 196616 | tf_op jit(solution)/shard_map/ppermute | solution.py:271
  205.2 2.3 collective-permute-done.37
  207.5 2.6 %collective-permute-done.39 = f32[64,256]{1,0:T(8,128)S(1)} collective-permute-done((f32[64,256]{1,0:T(8,128)S(1)}, f32[64,256]{1,0:T(8,128)S(1)}, u32[]{:S(2)}, u32[]{:S(2)}) %collective-permute-start.39) | collective-permute-done | bytes 65568 | tf_op jit(solution)/shard_map/ppermute | solution.py:271
  210.1 2.9 %collective-permute-done.41 = f32[2,384,384]{2,1,0:T(8,128)S(1)} collective-permute-done((f32[2,384,384]{2,1,0:T(8,128)S(1)}, f32[2,384,384]{2,1,0:T(8,128)S(1)}, u32[]{:S(2)}, u32[]{:S(2)}) %collective-permute-start.41) | collective-permute-done | bytes 1179680 | tf_op jit(solution)/shard_map/ppermute | solution.py:252
  213.0 2.4 collective-permute-start.43
  216.1 4.2 %collective-permute-done.42 = f32[64,256]{1,0:T(8,128)S(1)} collective-permute-done((f32[64,256]{1,0:T(8,128)S(1)}, f32[64,256]{1,0:T(8,128)S(1)}, u32[]{:S(2)}, u32[]{:S(2)}) %collective-permute-start.42) | collective-permute-done | bytes 65568 | tf_op jit(solution)/shard_map/ppermute | solution.py:271
  221.0 4.0 %collective-permute-start.45 = (f32[64,256]{1,0:T(8,128)S(1)}, f32[64,256]{1,0:T(8,128)S(1)}, u32[]{:S(2)}, u32[]{:S(2)}) collective-permute-start(f32[64,256]{1,0:T(8,128)S(1)} %get-tuple-element.85), channel_id=1, source_target_pairs={{0,2},{1,3},{2,4},{3,5},{4,6},{5,7},{6,0},{7,1},{16,18},{17,19},{1... | collective-permute-start | bytes 196616 | tf_op jit(solution)/shard_map/ppermute | solution.py:271
  225.1 14.4 %collective-permute-start.46 = (f32[64,256]{1,0:T(8,128)S(1)}, f32[64,256]{1,0:T(8,128)S(1)}, u32[]{:S(2)}, u32[]{:S(2)}) collective-permute-start(f32[64,256]{1,0:T(8,128)S(1)} %get-tuple-element.85), channel_id=1, source_target_pairs={{0,4},{1,5},{2,6},{3,7},{4,0},{5,1},{6,2},{7,3},{16,20},{17,21},{1... | collective-permute-start | bytes 196616 | tf_op jit(solution)/shard_map/ppermute | solution.py:271
  (156 shorter events, 47.0 us)
Async XLA Ops:
  2.0 9.7 %collective-permute-start.1 = (f32[2,128,256]{2,1,0:T(8,128)S(1)}, f32[2,128,256]{2,1,0:T(8,128)S(1)}, u32[]{:S(2)}, u32[]{:S(2)}) collective-permute-start(f32[2,128,256]{2,1,0:T(8,128)S(1)} %pad_maximum_fusion.13), channel_id=1, source_target_pairs={{0,112},{16,0},{32,16},{48,32},{64,48},{80,64},{96,80},{112,96},{1... | collective-permute-start | bytes 786440 | tf_op jit(solution)/shard_map/ppermute | solution.py:252
  6.7 15.9 %collective-permute-start = (f32[2,128,256]{2,1,0:T(8,128)S(1)}, f32[2,128,256]{2,1,0:T(8,128)S(1)}, u32[]{:S(2)}, u32[]{:S(2)}) collective-permute-start(f32[2,128,256]{2,1,0:T(8,128)S(1)} %pad_maximum_fusion.12), channel_id=1, source_target_pairs={{0,16},{16,32},{32,48},{48,64},{64,80},{80,96},{96,112},{112,0},{1... | collective-permute-start | bytes 786440 | tf_op jit(solution)/shard_map/ppermute | solution.py:252
  7.6 21.7 %collective-permute-start.2 = (f32[2,128,256]{2,1,0:T(8,128)}, f32[2,128,256]{2,1,0:T(8,128)S(1)}, u32[]{:S(2)}, u32[]{:S(2)}) collective-permute-start(f32[2,128,256]{2,1,0:T(8,128)} %get-tuple-element.96), channel_id=1, source_target_pairs={{0,16},{16,32},{32,48},{48,64},{64,80},{80,96},{96,112},{112,0},{1... | collective-permute-start | bytes 786440 | tf_op jit(solution)/shard_map/ppermute | solution.py:252
  7.8 21.6 %collective-permute-start.3 = (f32[2,128,256]{2,1,0:T(8,128)}, f32[2,128,256]{2,1,0:T(8,128)}, u32[]{:S(2)}, u32[]{:S(2)}) collective-permute-start(f32[2,128,256]{2,1,0:T(8,128)} %get-tuple-element.95), channel_id=1, source_target_pairs={{0,112},{16,0},{32,16},{48,32},{64,48},{80,64},{96,80},{112,96},{1... | collective-permute-start | bytes 786440 | tf_op jit(solution)/shard_map/ppermute | solution.py:252
  27.2 9.0 %collective-permute-start.6 = (f32[2,512,128]{2,1,0:T(8,128)S(1)}, f32[2,512,128]{2,1,0:T(8,128)}, u32[]{:S(2)}, u32[]{:S(2)}) collective-permute-start(f32[2,512,128]{2,1,0:T(8,128)S(1)} %get-tuple-element.93), channel_id=1, source_target_pairs={{0,15},{1,0},{2,1},{3,2},{4,3},{5,4},{6,5},{7,6},{8,7},{9,8},{10,9... | collective-permute-start | bytes 1572872 | tf_op jit(solution)/shard_map/ppermute | solution.py:252
  30.0 9.0 %collective-permute-start.7 = (f32[2,256,128]{2,1,0:T(8,128)}, f32[2,256,128]{2,1,0:T(8,128)}, u32[]{:S(2)}, u32[]{:S(2)}) collective-permute-start(f32[2,256,128]{2,1,0:T(8,128)} %pad_maximum_fusion.14), channel_id=1, source_target_pairs={{0,15},{1,0},{2,1},{3,2},{4,3},{5,4},{6,5},{7,6},{8,7},{9,8},{10,9... | collective-permute-start | bytes 786440 | tf_op jit(solution)/shard_map/ppermute | solution.py:252
  58.2 14.2 %collective-permute-start.10 = (f32[2,768,128]{2,1,0:T(8,128)}, f32[2,768,128]{2,1,0:T(8,128)}, u32[]{:S(2)}, u32[]{:S(2)}) collective-permute-start(f32[2,768,128]{2,1,0:T(8,128)} %get-tuple-element.49), channel_id=1, source_target_pairs={{0,1},{1,2},{2,3},{3,4},{4,5},{5,6},{6,7},{7,8},{8,9},{9,10},{10,1... | collective-permute-start | bytes 2359304 | tf_op jit(solution)/shard_map/ppermute | solution.py:252
  58.2 14.2 %collective-permute-start.9 = (f32[2,768,128]{2,1,0:T(8,128)}, f32[2,768,128]{2,1,0:T(8,128)}, u32[]{:S(2)}, u32[]{:S(2)}) collective-permute-start(f32[2,768,128]{2,1,0:T(8,128)} %get-tuple-element.48), channel_id=1, source_target_pairs={{0,15},{1,0},{2,1},{3,2},{4,3},{5,4},{6,5},{7,6},{8,7},{9,8},{10,9... | collective-permute-start | bytes 2359304 | tf_op jit(solution)/shard_map/ppermute | solution.py:252
  59.7 11.7 %collective-permute-start.8 = (f32[256,256]{1,0:T(8,128)S(1)}, f32[256,256]{1,0:T(8,128)S(1)}, u32[]{:S(2)}, u32[]{:S(2)}) collective-permute-start(f32[256,256]{1,0:T(8,128)S(1)} %dynamic-slice_bitcast_fusion.1), channel_id=1, source_target_pairs={{0,1},{1,0},{2,3},{3,2},{4,5},{5,4},{6,7},{7,6},{16,17},{17,16},{1... | collective-permute-start | bytes 786440 | tf_op jit(solution)/shard_map/ppermute | solution.py:271
  66.9 44.4 %collective-permute-start.14 = (f32[2,256,256]{2,1,0:T(8,128)}, f32[2,256,256]{2,1,0:T(8,128)S(1)}, u32[]{:S(2)}, u32[]{:S(2)}) collective-permute-start(f32[2,256,256]{2,1,0:T(8,128)} %get-tuple-element.61), channel_id=1, source_target_pairs={{0,112},{16,0},{32,16},{48,32},{64,48},{80,64},{96,80},{112,96},{1... | collective-permute-start | bytes 1572872 | tf_op jit(solution)/shard_map/ppermute | solution.py:252
  71.4 39.9 %collective-permute-start.15 = (f32[2,256,256]{2,1,0:T(8,128)}, f32[2,256,256]{2,1,0:T(8,128)S(1)}, u32[]{:S(2)}, u32[]{:S(2)}) collective-permute-start(f32[2,256,256]{2,1,0:T(8,128)} %get-tuple-element.64), channel_id=1, source_target_pairs={{0,16},{16,32},{32,48},{48,64},{64,80},{80,96},{96,112},{112,0},{1... | collective-permute-start | bytes 1572872 | tf_op jit(solution)/shard_map/ppermute | solution.py:252
  72.4 14.7 %collective-permute-start.11 = (f32[64,256]{1,0:T(8,128)S(1)}, f32[64,256]{1,0:T(8,128)S(1)}, u32[]{:S(2)}, u32[]{:S(2)}) collective-permute-start(f32[64,256]{1,0:T(8,128)S(1)} %get-tuple-element.119), channel_id=1, source_target_pairs={{0,2},{1,3},{2,4},{3,5},{4,6},{5,7},{6,0},{7,1},{16,18},{17,19},{1... | collective-permute-start | bytes 196616 | tf_op jit(solution)/shard_map/ppermute | solution.py:271
  72.8 22.0 %collective-permute-start.12 = (f32[64,256]{1,0:T(8,128)S(1)}, f32[64,256]{1,0:T(8,128)S(1)}, u32[]{:S(2)}, u32[]{:S(2)}) collective-permute-start(f32[64,256]{1,0:T(8,128)S(1)} %get-tuple-element.121), channel_id=1, source_target_pairs={{0,4},{1,5},{2,6},{3,7},{4,0},{5,1},{6,2},{7,3},{16,20},{17,21},{1... | collective-permute-start | bytes 196616 | tf_op jit(solution)/shard_map/ppermute | solution.py:271
  84.0 10.8 %collective-permute-start.13 = (f32[64,256]{1,0:T(8,128)S(1)}, f32[64,256]{1,0:T(8,128)S(1)}, u32[]{:S(2)}, u32[]{:S(2)}) collective-permute-start(f32[64,256]{1,0:T(8,128)S(1)} %get-tuple-element.120), channel_id=1, source_target_pairs={{0,6},{1,7},{2,0},{3,1},{4,2},{5,3},{6,4},{7,5},{16,22},{17,23},{1... | collective-permute-start | bytes 196616 | tf_op jit(solution)/shard_map/ppermute | solution.py:271
  87.1 33.9 %collective-permute-start.25 = (f32[2,256,256]{2,1,0:T(8,128)S(1)}, f32[2,256,256]{2,1,0:T(8,128)S(1)}, u32[]{:S(2)}, u32[]{:S(2)}) collective-permute-start(f32[2,256,256]{2,1,0:T(8,128)S(1)} %get-tuple-element.105), channel_id=1, source_target_pairs={{0,16},{16,32},{32,48},{48,64},{64,80},{80,96},{96,112},{112,0},{1... | collective-permute-start | bytes 1572872 | tf_op jit(solution)/shard_map/ppermute | solution.py:252
  94.8 27.8 %collective-permute-start.26 = (f32[2,256,256]{2,1,0:T(8,128)S(1)}, f32[2,256,256]{2,1,0:T(8,128)S(1)}, u32[]{:S(2)}, u32[]{:S(2)}) collective-permute-start(f32[2,256,256]{2,1,0:T(8,128)S(1)} %get-tuple-element.106), channel_id=1, source_target_pairs={{0,112},{16,0},{32,16},{48,32},{64,48},{80,64},{96,80},{112,96},{1... | collective-permute-start | bytes 1572872 | tf_op jit(solution)/shard_map/ppermute | solution.py:252
  117.5 9.1 %collective-permute-start.19 = (f32[64,256]{1,0:T(8,128)S(1)}, f32[64,256]{1,0:T(8,128)S(1)}, u32[]{:S(2)}, u32[]{:S(2)}) collective-permute-start(f32[64,256]{1,0:T(8,128)S(1)} %add_add_fusion.3), channel_id=1, source_target_pairs={{0,16},{1,17},{2,18},{3,19},{4,20},{5,21},{6,22},{7,23},{16,8},{17... | collective-permute-start | bytes 196616 | tf_op jit(solution)/shard_map/ppermute | solution.py:271
  125.4 17.7 %collective-permute-start.27 = (f32[2,768,128]{2,1,0:T(8,128)}, f32[2,768,128]{2,1,0:T(8,128)}, u32[]{:S(2)}, u32[]{:S(2)}) collective-permute-start(f32[2,768,128]{2,1,0:T(8,128)} %get-tuple-element.104), channel_id=1, source_target_pairs={{0,1},{1,2},{2,3},{3,4},{4,5},{5,6},{6,7},{7,8},{8,9},{9,10},{10,1... | collective-permute-start | bytes 2359304 | tf_op jit(solution)/shard_map/ppermute | solution.py:252
  125.4 17.7 %collective-permute-start.28 = (f32[2,768,128]{2,1,0:T(8,128)}, f32[2,768,128]{2,1,0:T(8,128)}, u32[]{:S(2)}, u32[]{:S(2)}) collective-permute-start(f32[2,768,128]{2,1,0:T(8,128)} %get-tuple-element.103), channel_id=1, source_target_pairs={{0,15},{1,0},{2,1},{3,2},{4,3},{5,4},{6,5},{7,6},{8,7},{9,8},{10,9... | collective-permute-start | bytes 2359304 | tf_op jit(solution)/shard_map/ppermute | solution.py:252
  126.7 15.5 %collective-permute-start.22 = (f32[64,256]{1,0:T(8,128)S(1)}, f32[64,256]{1,0:T(8,128)S(1)}, u32[]{:S(2)}, u32[]{:S(2)}) collective-permute-start(f32[64,256]{1,0:T(8,128)S(1)} %get-tuple-element.87), channel_id=1, source_target_pairs={{0,2},{1,3},{2,4},{3,5},{4,6},{5,7},{6,0},{7,1},{16,18},{17,19},{1... | collective-permute-start | bytes 196616 | tf_op jit(solution)/shard_map/ppermute | solution.py:271
  126.9 16.1 %collective-permute-start.23 = (f32[64,256]{1,0:T(8,128)S(1)}, f32[64,256]{1,0:T(8,128)S(1)}, u32[]{:S(2)}, u32[]{:S(2)}) collective-permute-start(f32[64,256]{1,0:T(8,128)S(1)} %get-tuple-element.87), channel_id=1, source_target_pairs={{0,4},{1,5},{2,6},{3,7},{4,0},{5,1},{6,2},{7,3},{16,20},{17,21},{1... | collective-permute-start | bytes 196616 | tf_op jit(solution)/shard_map/ppermute | solution.py:271
  131.4 11.6 %collective-permute-start.24 = (f32[64,256]{1,0:T(8,128)S(1)}, f32[64,256]{1,0:T(8,128)S(1)}, u32[]{:S(2)}, u32[]{:S(2)}) collective-permute-start(f32[64,256]{1,0:T(8,128)S(1)} %get-tuple-element.87), channel_id=1, source_target_pairs={{0,6},{1,7},{2,0},{3,1},{4,2},{5,3},{6,4},{7,5},{16,22},{17,23},{1... | collective-permute-start | bytes 196616 | tf_op jit(solution)/shard_map/ppermute | solution.py:271
  163.1 16.0 %collective-permute-start.31 = (f32[2,384,384]{2,1,0:T(8,128)S(1)}, f32[2,384,384]{2,1,0:T(8,128)S(1)}, u32[]{:S(2)}, u32[]{:S(2)}) collective-permute-start(f32[2,384,384]{2,1,0:T(8,128)S(1)} %get-tuple-element.69), channel_id=1, source_target_pairs={{0,15},{1,0},{2,1},{3,2},{4,3},{5,4},{6,5},{7,6},{8,7},{9,8},{10,9... | collective-permute-start | bytes 3538952 | tf_op jit(solution)/shard_map/ppermute | solution.py:252
  168.5 10.7 %collective-permute-start.32 = (f32[2,384,128]{2,1,0:T(8,128)S(1)}, f32[2,384,128]{2,1,0:T(8,128)S(1)}, u32[]{:S(2)}, u32[]{:S(2)}) collective-permute-start(f32[2,384,128]{2,1,0:T(8,128)S(1)} %get-tuple-element.70), channel_id=1, source_target_pairs={{0,112},{16,0},{32,16},{48,32},{64,48},{80,64},{96,80},{112,96},{1... | collective-permute-start | bytes 1179656 | tf_op jit(solution)/shard_map/ppermute | solution.py:252
  179.3 18.0 %collective-permute-start.36 = (f32[2,384,128]{2,1,0:T(8,128)S(1)}, f32[2,384,128]{2,1,0:T(8,128)S(1)}, u32[]{:S(2)}, u32[]{:S(2)}) collective-permute-start(f32[2,384,128]{2,1,0:T(8,128)S(1)} %get-tuple-element.102), channel_id=1, source_target_pairs={{0,112},{16,0},{32,16},{48,32},{64,48},{80,64},{96,80},{112,96},{1... | collective-permute-start | bytes 1179656 | tf_op jit(solution)/shard_map/ppermute | solution.py:252
  183.2 10.4 %collective-permute-start.33 = (f32[64,256]{1,0:T(8,128)S(1)}, f32[64,256]{1,0:T(8,128)S(1)}, u32[]{:S(2)}, u32[]{:S(2)}) collective-permute-start(f32[64,256]{1,0:T(8,128)S(1)} %get-tuple-element.116), channel_id=1, source_target_pairs={{0,2},{1,3},{2,4},{3,5},{4,6},{5,7},{6,0},{7,1},{16,18},{17,19},{1... | collective-permute-start | bytes 196616 | tf_op jit(solution)/shard_map/ppermute | solution.py:271
  183.5 12.1 %collective-permute-start.34 = (f32[64,256]{1,0:T(8,128)S(1)}, f32[64,256]{1,0:T(8,128)S(1)}, u32[]{:S(2)}, u32[]{:S(2)}) collective-permute-start(f32[64,256]{1,0:T(8,128)S(1)} %get-tuple-element.118), channel_id=1, source_target_pairs={{0,4},{1,5},{2,6},{3,7},{4,0},{5,1},{6,2},{7,3},{16,20},{17,21},{1... | collective-permute-start | bytes 196616 | tf_op jit(solution)/shard_map/ppermute | solution.py:271
  197.3 15.7 %collective-permute-start.41 = (f32[2,384,384]{2,1,0:T(8,128)S(1)}, f32[2,384,384]{2,1,0:T(8,128)S(1)}, u32[]{:S(2)}, u32[]{:S(2)}) collective-permute-start(f32[2,384,384]{2,1,0:T(8,128)S(1)} %get-tuple-element.76), channel_id=1, source_target_pairs={{0,15},{1,0},{2,1},{3,2},{4,3},{5,4},{6,5},{7,6},{8,7},{9,8},{10,9... | collective-permute-start | bytes 3538952 | tf_op jit(solution)/shard_map/ppermute | solution.py:252
  199.6 10.4 %collective-permute-start.40 = (f32[2,384,128]{2,1,0:T(8,128)S(1)}, f32[2,384,128]{2,1,0:T(8,128)S(1)}, u32[]{:S(2)}, u32[]{:S(2)}) collective-permute-start(f32[2,384,128]{2,1,0:T(8,128)S(1)} %get-tuple-element.101), channel_id=1, source_target_pairs={{0,112},{16,0},{32,16},{48,32},{64,48},{80,64},{96,80},{112,96},{1... | collective-permute-start | bytes 1179656 | tf_op jit(solution)/shard_map/ppermute | solution.py:252
  207.5 35.4 %collective-permute-start.48 = (f32[2,384,128]{2,1,0:T(8,128)S(1)}, f32[2,384,128]{2,1,0:T(8,128)S(1)}, u32[]{:S(2)}, u32[]{:S(2)}) collective-permute-start(f32[2,384,128]{2,1,0:T(8,128)S(1)} %get-tuple-element.107), channel_id=1, source_target_pairs={{0,112},{16,0},{32,16},{48,32},{64,48},{80,64},{96,80},{112,96},{1... | collective-permute-start | bytes 1179656 | tf_op jit(solution)/shard_map/ppermute | solution.py:252
  221.0 19.3 %collective-permute-start.45 = (f32[64,256]{1,0:T(8,128)S(1)}, f32[64,256]{1,0:T(8,128)S(1)}, u32[]{:S(2)}, u32[]{:S(2)}) collective-permute-start(f32[64,256]{1,0:T(8,128)S(1)} %get-tuple-element.85), channel_id=1, source_target_pairs={{0,2},{1,3},{2,4},{3,5},{4,6},{5,7},{6,0},{7,1},{16,18},{17,19},{1... | collective-permute-start | bytes 196616 | tf_op jit(solution)/shard_map/ppermute | solution.py:271
  225.1 17.2 %collective-permute-start.46 = (f32[64,256]{1,0:T(8,128)S(1)}, f32[64,256]{1,0:T(8,128)S(1)}, u32[]{:S(2)}, u32[]{:S(2)}) collective-permute-start(f32[64,256]{1,0:T(8,128)S(1)} %get-tuple-element.85), channel_id=1, source_target_pairs={{0,4},{1,5},{2,6},{3,7},{4,0},{5,1},{6,2},{7,3},{16,20},{17,21},{1... | collective-permute-start | bytes 196616 | tf_op jit(solution)/shard_map/ppermute | solution.py:271
  (34 other events, 288.6 us)
where the time goes:
time: 249 us; the launch traced here: 248 us
  starting transfers between devices  115 us (46%)
  waiting for transfers between devices  74.7 us (30%)
  Pallas kernels  34.8 us (14%)
  other arithmetic  12.6 us (5%)
  local copies, waits for them, and re-layouts  9.03 us (4%)
    ppermute x28, starting transfers between devices, moved(): return lax.ppermute(array, ('row', 'col'), pairs)  74.1 us
    ppermute x22, waiting for transfers between devices, shifted(): lax.ppermute(array, axis, [(i, (i + by) % count) for i in range(count)])  45.1 us
    ppermute x22, starting transfers between devices, shifted(): lax.ppermute(array, axis, [(i, (i + by) % count) for i in range(count)])  41 us
    pallas_call x2, Pallas kernels, frames(): pl.pallas_call(kernel, out_shape=out_shapes, in_specs=[smem] + [anywhere]...  34.8 us
    ppermute x28, waiting for transfers between devices, moved(): return lax.ppermute(array, ('row', 'col'), pairs)  29.6 us
  transfers between devices with their start and end apart: 50, of which 23 were waited for; matrix products, arithmetic and copies ran while one was open for 7% of the time, Pallas kernels for 0%

commit v1 on v0

--- a/solution.py
+++ b/solution.py
@@ -271,25 +271,24 @@
     return lax.ppermute(array, ("row", "col"), pairs)
 
 
-def core_and_y():
-    col = lax.axis_index("col")
-    return (col % 2, col // 2 % (lax.axis_size("col") // 4), lax.axis_size("col") // 4)
+def core_and_x():
+    return (lax.axis_index("col") % 2, lax.axis_index("row") // 2, lax.axis_size("row") // 2)
 
 
 def core_share(part):
-    core, _, _ = core_and_y()
+    core, _, _ = core_and_x()
     halves = part.reshape(2, -1, part.shape[-1])
     mine = lax.dynamic_index_in_dim(halves, core, 0, False)
     other = lax.dynamic_index_in_dim(halves, 1 - core, 0, False)
     return mine + moved(other, "core", 1)
 
 
-def y_share(half):
-    _, y, y_count = core_and_y()
-    quarters = half.reshape(y_count, -1, half.shape[-1])
-    total = lax.dynamic_index_in_dim(quarters, y, 0, False)
+def x_share(half):
+    _, x, x_count = core_and_x()
+    parts = half.reshape(x_count, -1, half.shape[-1])
+    total = lax.dynamic_index_in_dim(parts, x, 0, False)
     arrived = [
-        moved(lax.dynamic_index_in_dim(quarters, (y + by) % y_count, 0, False), "y", by) for by in range(1, y_count)
+        moved(lax.dynamic_index_in_dim(parts, (x + by) % x_count, 0, False), "x", by) for by in range(1, x_count)
     ]
     for value in arrived:
         total = total + value
@@ -302,17 +301,17 @@
     return total
 
 
-def y_gathered(total):
-    _, y, y_count = core_and_y()
-    gathered = [total] + [moved(total, "y", by) for by in range(1, y_count)]
-    half = jnp.zeros((y_count, *total.shape), jnp.float32)
+def x_gathered(total):
+    _, x, x_count = core_and_x()
+    gathered = [total] + [moved(total, "x", by) for by in range(1, x_count)]
+    half = jnp.zeros((x_count, *total.shape), jnp.float32)
     for by, value in enumerate(gathered):
-        half = lax.dynamic_update_index_in_dim(half, value, (y - by) % y_count, 0)
+        half = lax.dynamic_update_index_in_dim(half, value, (x - by) % x_count, 0)
     return half
 
 
 def both_halves(half, shape):
-    core, _, _ = core_and_y()
+    core, _, _ = core_and_x()
     other = moved(half, "core", 1)
     first = jnp.where(core == 0, half, other)
     second = jnp.where(core == 0, other, half)
@@ -383,21 +382,21 @@
         info, placed, probe, intensity, mats, full, cuts, False
     )
 
-    x_count = lax.axis_size("row") // 2
+    y_count = lax.axis_size("col") // 4
     inner_up = shifted(inner_top, "row", -1)
     inner_down = shifted(inner_low, "row", 1)
     from_right = shifted(grad_left, "col", -1)
     from_left = shifted(grad_right, "col", 1)
-    share = core_share(probe_part)
+    share = x_share(core_share(probe_part))
     share, from_right, from_left, edges, inner_top, inner_low, inner_mid = lax.optimization_barrier(
         (share, from_right, from_left, edges, inner_top, inner_low, inner_mid)
     )
     edges = edges + jnp.concatenate([from_left, from_right], axis=2)
     edges_up = shifted(edges[:, :side], "row", -1)
     edges_down = shifted(edges[:, tile:], "row", 1)
-    share = y_share(share)
+    share = sum_along(share, "y", y_count)
     share, inner_up, inner_down = lax.optimization_barrier((share, inner_up, inner_down))
-    half_sum = y_gathered(sum_along(sum_along(share, "x", x_count), "z", 4))
+    half_sum = x_gathered(sum_along(share, "z", 4))
     old_edges = jnp.concatenate([above_outer, outer(object_field), below_outer], axis=1)
     new_edges = jnp.concatenate(
         [
@@ -442,17 +441,15 @@
 
     up_0 = shifted(here_0, "row", -1)
     got_top = shifted(out_top, "col", -1)
-    share = core_share(probe_part)
+    share = x_share(core_share(probe_part))
     share, got_top, up_0 = lax.optimization_barrier((share, got_top, up_0))
     up_1 = shifted(here_1[:, :, :width] + got_top[:, :, :width], "row", -1)
     up_2 = shifted(here_1[:, :, width:] + got_top[:, :, width : 2 * width], "row", -1)
     up_3 = shifted(got_top[:, :, 2 * width :], "row", -1)
-    share = y_share(share)
-    share, out_rest, up_1 = lax.optimization_barrier((share, out_rest, up_1))
+    share = sum_along(share, "y", y_count)
+    share, up_1, up_2, out_rest = lax.optimization_barrier((share, up_1, up_2, out_rest))
     got_rest = shifted(out_rest, "col", -1)
-    share = sum_along(share, "x", x_count)
-    share, up_2, got_rest = lax.optimization_barrier((share, up_2, got_rest))
-    half_sum = y_gathered(sum_along(share, "z", 4))
+    half_sum = x_gathered(sum_along(share, "z", 4))
     half_sum, up_3 = lax.optimization_barrier((half_sum, up_3))
     probe_total = both_halves(half_sum, probe.shape)
     mine = jnp.concatenate(

time: 249 us -> 250 us (level)
  the two profiles are of different devices: /device:TPU:1 before, /device:TPU:24 now
where the time goes in v1:
time: 250 us; the launch traced here: 255 us
  starting transfers between devices  112 us (45%)
  waiting for transfers between devices  85.6 us (34%)
  Pallas kernels  34.9 us (14%)
  other arithmetic  12.4 us (5%)
  local copies, waits for them, and re-layouts  8.23 us (3%)
    ppermute x28, starting transfers between devices, moved(): return lax.ppermute(array, ('row', 'col'), pairs)  69.7 us
    ppermute x22, waiting for transfers between devices, shifted(): lax.ppermute(array, axis, [(i, (i + by) % count) for i in range(count)])  49.7 us
    ppermute x22, starting transfers between devices, shifted(): lax.ppermute(array, axis, [(i, (i + by) % count) for i in range(count)])  42.8 us
    ppermute x28, waiting for transfers between devices, moved(): return lax.ppermute(array, ('row', 'col'), pairs)  35.9 us
    pallas_call x2, Pallas kernels, frames(): pl.pallas_call(kernel, out_shape=out_shapes, in_specs=[smem] + [anywhere]...  34.9 us
  transfers between devices with their start and end apart: 50, of which 28 were waited for; matrix products, arithmetic and copies ran while one was open for 6% of the time, Pallas kernels for 0%

profile of v1, /device:TPU:24, one launch (start us, length us, event | category | flops | bytes accessed | tf_op | source)
XLA Modules:
  0.0 254.8 jit_solution(10215519144343018301)
XLA Ops:
  2.0 4.2 %collective-permute-start.1 = (f32[2,128,256]{2,1,0:T(8,128)S(1)}, f32[2,128,256]{2,1,0:T(8,128)S(1)}, u32[]{:S(2)}, u32[]{:S(2)}) collective-permute-start(f32[2,128,256]{2,1,0:T(8,128)S(1)} %pad_maximum_fusion.13), channel_id=1, source_target_pairs={{0,112},{16,0},{32,16},{48,32},{64,48},{80,64},{96,80},{112,96},{1... | collective-permute-start | bytes 786440 | tf_op jit(solution)/shard_map/ppermute | solution.py:252
  7.8 3.4 %collective-permute-start.3 = (f32[2,128,256]{2,1,0:T(8,128)}, f32[2,128,256]{2,1,0:T(8,128)}, u32[]{:S(2)}, u32[]{:S(2)}) collective-permute-start(f32[2,128,256]{2,1,0:T(8,128)} %get-tuple-element.91), channel_id=1, source_target_pairs={{0,112},{16,0},{32,16},{48,32},{64,48},{80,64},{96,80},{112,96},{1... | collective-permute-start | bytes 786440 | tf_op jit(solution)/shard_map/ppermute | solution.py:252
  11.2 10.9 %collective-permute-done.1.refs_4_ = f32[2,128,256]{2,1,0:T(8,128)S(1)} collective-permute-done((f32[2,128,256]{2,1,0:T(8,128)S(1)}, f32[2,128,256]{2,1,0:T(8,128)S(1)}, u32[]{:S(2)}, u32[]{:S(2)}) %collective-permute-start.1) | collective-permute-done | bytes 262176 | tf_op jit(solution)/shard_map/ppermute | solution.py:252
  24.5 3.6 %collective-permute-start.5 = (f32[2,512,128]{2,1,0:T(8,128)}, f32[2,512,128]{2,1,0:T(8,128)S(1)}, u32[]{:S(2)}, u32[]{:S(2)}) collective-permute-start(f32[2,512,128]{2,1,0:T(8,128)} %get-tuple-element.90), channel_id=1, source_target_pairs={{0,1},{1,2},{2,3},{3,4},{4,5},{5,6},{6,7},{7,8},{8,9},{9,10},{10,1... | collective-permute-start | bytes 1572872 | tf_op jit(solution)/shard_map/ppermute | solution.py:252
  30.6 4.7 %collective-permute-done.5.refs_6_ = f32[2,512,128]{2,1,0:T(8,128)S(1)} collective-permute-done((f32[2,512,128]{2,1,0:T(8,128)}, f32[2,512,128]{2,1,0:T(8,128)S(1)}, u32[]{:S(2)}, u32[]{:S(2)}) %collective-permute-start.5) | collective-permute-done | bytes 524320 | tf_op jit(solution)/shard_map/ppermute | solution.py:252
  35.3 2.4 collective-permute-done.7.refs_9_
  37.7 19.2 %frames.2 = (f32[2,768,128]{2,1,0:T(8,128)}, f32[2,768,128]{2,1,0:T(8,128)}, f32[2,256,256]{2,1,0:T(8,128)}, f32[2,256,256]{2,1,0:T(8,128)}, f32[2,256,256]{2,1,...) custom-call(s32[12,3]{1,0:T(8,128)} %copy.13.refs_0_, f32[2,128,256]{2,1,0:T(8,128)} %copy-done.6, ...), custom_call_target="tpu_custom_call" | custom-call | tf_op jit(solution)/shard_map/frames/pallas_call | solution.py:227
  57.9 5.9 %collective-permute-start.8 = (f32[256,256]{1,0:T(8,128)S(1)}, f32[256,256]{1,0:T(8,128)S(1)}, u32[]{:S(2)}, u32[]{:S(2)}) collective-permute-start(f32[256,256]{1,0:T(8,128)S(1)} %dynamic-slice_bitcast_fusion.1), channel_id=1, source_target_pairs={{0,1},{1,0},{2,3},{3,2},{4,5},{5,4},{6,7},{7,6},{16,17},{17,16},{1... | collective-permute-start | bytes 786440 | tf_op jit(solution)/shard_map/ppermute | solution.py:271
  66.1 3.0 %collective-permute-start.11 = (f32[64,256]{1,0:T(8,128)S(1)}, f32[64,256]{1,0:T(8,128)S(1)}, u32[]{:S(2)}, u32[]{:S(2)}) collective-permute-start(f32[64,256]{1,0:T(8,128)S(1)} %get-tuple-element.116), channel_id=1, source_target_pairs={{0,96},{1,97},{2,98},{3,99},{4,100},{5,101},{6,102},{7,103},{16,11... | collective-permute-start | bytes 196616 | tf_op jit(solution)/shard_map/ppermute | solution.py:271
  71.8 3.7 %collective-permute-start.17 = (f32[2,256,256]{2,1,0:T(8,128)}, f32[2,256,256]{2,1,0:T(8,128)S(1)}, u32[]{:S(2)}, u32[]{:S(2)}) collective-permute-start(f32[2,256,256]{2,1,0:T(8,128)} %get-tuple-element.59), channel_id=1, source_target_pairs={{0,112},{16,0},{32,16},{48,32},{64,48},{80,64},{96,80},{112,96},{1... | collective-permute-start | bytes 1572872 | tf_op jit(solution)/shard_map/ppermute | solution.py:252
  75.6 3.0 %collective-permute-start.14 = (f32[64,256]{1,0:T(8,128)S(1)}, f32[64,256]{1,0:T(8,128)S(1)}, u32[]{:S(2)}, u32[]{:S(2)}) collective-permute-start(f32[64,256]{1,0:T(8,128)S(1)} %fusion.10), channel_id=1, source_target_pairs={{0,2},{1,3},{2,4},{3,5},{4,6},{5,7},{6,0},{7,1},{16,18},{17,19},{1... | collective-permute-start | bytes 196616 | tf_op jit(solution)/shard_map/ppermute | solution.py:271
  79.6 2.1 maximum_add_fusion
  81.8 6.7 %collective-permute-start.25 = (f32[2,256,256]{2,1,0:T(8,128)S(1)}, f32[2,256,256]{2,1,0:T(8,128)S(1)}, u32[]{:S(2)}, u32[]{:S(2)}) collective-permute-start(f32[2,256,256]{2,1,0:T(8,128)S(1)} %get-tuple-element.101), channel_id=1, source_target_pairs={{0,16},{16,32},{32,48},{48,64},{64,80},{80,96},{96,112},{112,0},{1... | collective-permute-start | bytes 1572872 | tf_op jit(solution)/shard_map/ppermute | solution.py:252
  88.5 7.8 %collective-permute-start.26 = (f32[2,256,256]{2,1,0:T(8,128)S(1)}, f32[2,256,256]{2,1,0:T(8,128)S(1)}, u32[]{:S(2)}, u32[]{:S(2)}) collective-permute-start(f32[2,256,256]{2,1,0:T(8,128)S(1)} %get-tuple-element.102), channel_id=1, source_target_pairs={{0,112},{16,0},{32,16},{48,32},{64,48},{80,64},{96,80},{112,96},{1... | collective-permute-start | bytes 1572872 | tf_op jit(solution)/shard_map/ppermute | solution.py:252
  96.4 13.9 %collective-permute-done.17 = f32[2,256,256]{2,1,0:T(8,128)S(1)} collective-permute-done((f32[2,256,256]{2,1,0:T(8,128)}, f32[2,256,256]{2,1,0:T(8,128)S(1)}, u32[]{:S(2)}, u32[]{:S(2)}) %collective-permute-start.17) | collective-permute-done | bytes 524320 | tf_op jit(solution)/shard_map/ppermute | solution.py:252
  111.9 3.4 %collective-permute-start.20 = (f32[64,256]{1,0:T(8,128)S(1)}, f32[64,256]{1,0:T(8,128)S(1)}, u32[]{:S(2)}, u32[]{:S(2)}) collective-permute-start(f32[64,256]{1,0:T(8,128)S(1)} %add_add_fusion.3), channel_id=1, source_target_pairs={{0,8},{1,9},{2,10},{3,11},{4,12},{5,13},{6,14},{7,15},{16,24},{17,... | collective-permute-start | bytes 196616 | tf_op jit(solution)/shard_map/ppermute | solution.py:271
  115.3 2.6 %collective-permute-start.21 = (f32[64,256]{1,0:T(8,128)S(1)}, f32[64,256]{1,0:T(8,128)S(1)}, u32[]{:S(2)}, u32[]{:S(2)}) collective-permute-start(f32[64,256]{1,0:T(8,128)S(1)} %add_add_fusion.3), channel_id=1, source_target_pairs={{0,24},{1,25},{2,26},{3,27},{4,28},{5,29},{6,30},{7,31},{16,0},{17... | collective-permute-start | bytes 196616 | tf_op jit(solution)/shard_map/ppermute | solution.py:271
  128.3 3.2 %collective-permute-start.23 = (f32[64,256]{1,0:T(8,128)S(1)}, f32[64,256]{1,0:T(8,128)S(1)}, u32[]{:S(2)}, u32[]{:S(2)}) collective-permute-start(f32[64,256]{1,0:T(8,128)S(1)} %get-tuple-element.83), channel_id=1, source_target_pairs={{0,64},{1,65},{2,66},{3,67},{4,68},{5,69},{6,70},{7,71},{16,80},{1... | collective-permute-start | bytes 196616 | tf_op jit(solution)/shard_map/ppermute | solution.py:271
  136.1 10.2 %collective-permute-start.29 = (f32[4,64,256]{2,1,0:T(8,128)S(1)}, f32[4,64,256]{2,1,0:T(8,128)}, u32[]{:S(2)}, u32[]{:S(2)}) collective-permute-start(f32[4,64,256]{2,1,0:T(8,128)S(1)} %bitcast_dynamic-update-slice_fusion.4), channel_id=1, source_target_pairs={{0,1},{1,0},{2,3},{3,2},{4,5},{5,4},{6,7},{7,6},{16,17},{17,16},{1... | collective-permute-start | bytes 786440 | tf_op jit(solution)/shard_map/ppermute | solution.py:271
  149.8 15.7 %frames.3 = (f32[2,384,384]{2,1,0:T(8,128)S(1)}, f32[2,384,384]{2,1,0:T(8,128)S(1)}, f32[2,384,128]{2,1,0:T(8,128)S(1)}, f32[2,384,256]{2,1,0:T(8,128)S(1)}, f32...) custom-call(s32[12,3]{1,0:T(8,128)S(1)} %copy-done.2, f32[2,768,128]{2,1,0:T(8,128)} %collective-permute-done.27.refs_1_, ...), custom_call_target="tpu_custom_call" | custom-call | tf_op jit(solution)/shard_map/frames/pallas_call | solution.py:227
  168.9 4.6 %collective-permute-start.32 = (f32[64,256]{1,0:T(8,128)S(1)}, f32[64,256]{1,0:T(8,128)S(1)}, u32[]{:S(2)}, u32[]{:S(2)}) collective-permute-start(f32[64,256]{1,0:T(8,128)S(1)} %get-tuple-element.114), channel_id=1, source_target_pairs={{0,64},{1,65},{2,66},{3,67},{4,68},{5,69},{6,70},{7,71},{16,80},{1... | collective-permute-start | bytes 196616 | tf_op jit(solution)/shard_map/ppermute | solution.py:271
  174.5 2.6 %collective-permute-done.32 = f32[64,256]{1,0:T(8,128)S(1)} collective-permute-done((f32[64,256]{1,0:T(8,128)S(1)}, f32[64,256]{1,0:T(8,128)S(1)}, u32[]{:S(2)}, u32[]{:S(2)}) %collective-permute-start.32) | collective-permute-done | bytes 65568 | tf_op jit(solution)/shard_map/ppermute | solution.py:271
  177.1 11.4 %collective-permute-done.33 = f32[64,256]{1,0:T(8,128)S(1)} collective-permute-done((f32[64,256]{1,0:T(8,128)S(1)}, f32[64,256]{1,0:T(8,128)S(1)}, u32[]{:S(2)}, u32[]{:S(2)}) %collective-permute-start.33) | collective-permute-done | bytes 65568 | tf_op jit(solution)/shard_map/ppermute | solution.py:271
  190.0 2.2 collective-permute-start.39
  192.2 2.5 collective-permute-start.40
  196.8 2.2 collective-permute-done.36
  201.8 8.3 %collective-permute-done.40 = f32[2,384,128]{2,1,0:T(8,128)S(1)} collective-permute-done((f32[2,384,128]{2,1,0:T(8,128)S(1)}, f32[2,384,128]{2,1,0:T(8,128)S(1)}, u32[]{:S(2)}, u32[]{:S(2)}) %collective-permute-start.40) | collective-permute-done | bytes 393248 | tf_op jit(solution)/shard_map/ppermute | solution.py:252
  213.3 4.0 %collective-permute-start.48 = (f32[2,384,128]{2,1,0:T(8,128)S(1)}, f32[2,384,128]{2,1,0:T(8,128)S(1)}, u32[]{:S(2)}, u32[]{:S(2)}) collective-permute-start(f32[2,384,128]{2,1,0:T(8,128)S(1)} %get-tuple-element.103), channel_id=1, source_target_pairs={{0,112},{16,0},{32,16},{48,32},{64,48},{80,64},{96,80},{112,96},{1... | collective-permute-start | bytes 1179656 | tf_op jit(solution)/shard_map/ppermute | solution.py:252
  218.6 20.5 %collective-permute-start.45 = (f32[64,256]{1,0:T(8,128)S(1)}, f32[64,256]{1,0:T(8,128)S(1)}, u32[]{:S(2)}, u32[]{:S(2)}) collective-permute-start(f32[64,256]{1,0:T(8,128)S(1)} %get-tuple-element.81), channel_id=1, source_target_pairs={{0,32},{1,33},{2,34},{3,35},{4,36},{5,37},{6,38},{7,39},{16,48},{1... | collective-permute-start | bytes 196616 | tf_op jit(solution)/shard_map/ppermute | solution.py:271
  239.3 2.7 %collective-permute-start.47 = (f32[64,256]{1,0:T(8,128)S(1)}, f32[64,256]{1,0:T(8,128)S(1)}, u32[]{:S(2)}, u32[]{:S(2)}) collective-permute-start(f32[64,256]{1,0:T(8,128)S(1)} %get-tuple-element.81), channel_id=1, source_target_pairs={{0,96},{1,97},{2,98},{3,99},{4,100},{5,101},{6,102},{7,103},{16,11... | collective-permute-start | bytes 196616 | tf_op jit(solution)/shard_map/ppermute | solution.py:271
  242.0 3.2 %collective-permute-done.46 = f32[64,256]{1,0:T(8,128)S(1)} collective-permute-done((f32[64,256]{1,0:T(8,128)S(1)}, f32[64,256]{1,0:T(8,128)S(1)}, u32[]{:S(2)}, u32[]{:S(2)}) %collective-permute-start.46) | collective-permute-done | bytes 65568 | tf_op jit(solution)/shard_map/ppermute | solution.py:271
  247.8 5.1 %collective-permute-done.41 = f32[2,384,384]{2,1,0:T(8,128)S(1)} collective-permute-done((f32[2,384,384]{2,1,0:T(8,128)S(1)}, f32[2,384,384]{2,1,0:T(8,128)S(1)}, u32[]{:S(2)}, u32[]{:S(2)}) %collective-permute-start.41) | collective-permute-done | bytes 1179680 | tf_op jit(solution)/shard_map/ppermute | solution.py:252
  (160 shorter events, 54.6 us)
Async XLA Ops:
  2.0 20.1 %collective-permute-start.1 = (f32[2,128,256]{2,1,0:T(8,128)S(1)}, f32[2,128,256]{2,1,0:T(8,128)S(1)}, u32[]{:S(2)}, u32[]{:S(2)}) collective-permute-start(f32[2,128,256]{2,1,0:T(8,128)S(1)} %pad_maximum_fusion.13), channel_id=1, source_target_pairs={{0,112},{16,0},{32,16},{48,32},{64,48},{80,64},{96,80},{112,96},{1... | collective-permute-start | bytes 786440 | tf_op jit(solution)/shard_map/ppermute | solution.py:252
  6.2 16.0 %collective-permute-start = (f32[2,128,256]{2,1,0:T(8,128)S(1)}, f32[2,128,256]{2,1,0:T(8,128)S(1)}, u32[]{:S(2)}, u32[]{:S(2)}) collective-permute-start(f32[2,128,256]{2,1,0:T(8,128)S(1)} %pad_maximum_fusion.12), channel_id=1, source_target_pairs={{0,16},{16,32},{32,48},{48,64},{64,80},{80,96},{96,112},{112,0},{1... | collective-permute-start | bytes 786440 | tf_op jit(solution)/shard_map/ppermute | solution.py:252
  7.1 22.6 %collective-permute-start.2 = (f32[2,128,256]{2,1,0:T(8,128)}, f32[2,128,256]{2,1,0:T(8,128)S(1)}, u32[]{:S(2)}, u32[]{:S(2)}) collective-permute-start(f32[2,128,256]{2,1,0:T(8,128)} %get-tuple-element.92), channel_id=1, source_target_pairs={{0,16},{16,32},{32,48},{48,64},{64,80},{80,96},{96,112},{112,0},{1... | collective-permute-start | bytes 786440 | tf_op jit(solution)/shard_map/ppermute | solution.py:252
  7.8 21.9 %collective-permute-start.3 = (f32[2,128,256]{2,1,0:T(8,128)}, f32[2,128,256]{2,1,0:T(8,128)}, u32[]{:S(2)}, u32[]{:S(2)}) collective-permute-start(f32[2,128,256]{2,1,0:T(8,128)} %get-tuple-element.91), channel_id=1, source_target_pairs={{0,112},{16,0},{32,16},{48,32},{64,48},{80,64},{96,80},{112,96},{1... | collective-permute-start | bytes 786440 | tf_op jit(solution)/shard_map/ppermute | solution.py:252
  24.5 10.8 %collective-permute-start.5 = (f32[2,512,128]{2,1,0:T(8,128)}, f32[2,512,128]{2,1,0:T(8,128)S(1)}, u32[]{:S(2)}, u32[]{:S(2)}) collective-permute-start(f32[2,512,128]{2,1,0:T(8,128)} %get-tuple-element.90), channel_id=1, source_target_pairs={{0,1},{1,2},{2,3},{3,4},{4,5},{5,6},{6,7},{7,8},{8,9},{9,10},{10,1... | collective-permute-start | bytes 1572872 | tf_op jit(solution)/shard_map/ppermute | solution.py:252
  29.8 8.0 %collective-permute-start.7 = (f32[2,256,128]{2,1,0:T(8,128)}, f32[2,256,128]{2,1,0:T(8,128)}, u32[]{:S(2)}, u32[]{:S(2)}) collective-permute-start(f32[2,256,128]{2,1,0:T(8,128)} %pad_maximum_fusion.14), channel_id=1, source_target_pairs={{0,15},{1,0},{2,1},{3,2},{4,3},{5,4},{6,5},{7,6},{8,7},{9,8},{10,9... | collective-permute-start | bytes 786440 | tf_op jit(solution)/shard_map/ppermute | solution.py:252
  63.8 11.8 %collective-permute-start.12 = (f32[2,768,128]{2,1,0:T(8,128)}, f32[2,768,128]{2,1,0:T(8,128)}, u32[]{:S(2)}, u32[]{:S(2)}) collective-permute-start(f32[2,768,128]{2,1,0:T(8,128)} %get-tuple-element.46), channel_id=1, source_target_pairs={{0,15},{1,0},{2,1},{3,2},{4,3},{5,4},{6,5},{7,6},{8,7},{9,8},{10,9... | collective-permute-start | bytes 2359304 | tf_op jit(solution)/shard_map/ppermute | solution.py:252
  63.8 11.8 %collective-permute-start.13 = (f32[2,768,128]{2,1,0:T(8,128)}, f32[2,768,128]{2,1,0:T(8,128)}, u32[]{:S(2)}, u32[]{:S(2)}) collective-permute-start(f32[2,768,128]{2,1,0:T(8,128)} %get-tuple-element.47), channel_id=1, source_target_pairs={{0,1},{1,2},{2,3},{3,4},{4,5},{5,6},{6,7},{7,8},{8,9},{9,10},{10,1... | collective-permute-start | bytes 2359304 | tf_op jit(solution)/shard_map/ppermute | solution.py:252
  66.1 9.5 %collective-permute-start.11 = (f32[64,256]{1,0:T(8,128)S(1)}, f32[64,256]{1,0:T(8,128)S(1)}, u32[]{:S(2)}, u32[]{:S(2)}) collective-permute-start(f32[64,256]{1,0:T(8,128)S(1)} %get-tuple-element.116), channel_id=1, source_target_pairs={{0,96},{1,97},{2,98},{3,99},{4,100},{5,101},{6,102},{7,103},{16,11... | collective-permute-start | bytes 196616 | tf_op jit(solution)/shard_map/ppermute | solution.py:271
  71.8 38.5 %collective-permute-start.17 = (f32[2,256,256]{2,1,0:T(8,128)}, f32[2,256,256]{2,1,0:T(8,128)S(1)}, u32[]{:S(2)}, u32[]{:S(2)}) collective-permute-start(f32[2,256,256]{2,1,0:T(8,128)} %get-tuple-element.59), channel_id=1, source_target_pairs={{0,112},{16,0},{32,16},{48,32},{64,48},{80,64},{96,80},{112,96},{1... | collective-permute-start | bytes 1572872 | tf_op jit(solution)/shard_map/ppermute | solution.py:252
  75.6 34.8 %collective-permute-start.18 = (f32[2,256,256]{2,1,0:T(8,128)}, f32[2,256,256]{2,1,0:T(8,128)S(1)}, u32[]{:S(2)}, u32[]{:S(2)}) collective-permute-start(f32[2,256,256]{2,1,0:T(8,128)} %get-tuple-element.62), channel_id=1, source_target_pairs={{0,16},{16,32},{32,48},{48,64},{64,80},{80,96},{96,112},{112,0},{1... | collective-permute-start | bytes 1572872 | tf_op jit(solution)/shard_map/ppermute | solution.py:252
  78.7 9.9 %collective-permute-start.15 = (f32[64,256]{1,0:T(8,128)S(1)}, f32[64,256]{1,0:T(8,128)S(1)}, u32[]{:S(2)}, u32[]{:S(2)}) collective-permute-start(f32[64,256]{1,0:T(8,128)S(1)} %fusion.10), channel_id=1, source_target_pairs={{0,4},{1,5},{2,6},{3,7},{4,0},{5,1},{6,2},{7,3},{16,20},{17,21},{1... | collective-permute-start | bytes 196616 | tf_op jit(solution)/shard_map/ppermute | solution.py:271
  78.7 17.7 %collective-permute-start.16 = (f32[64,256]{1,0:T(8,128)S(1)}, f32[64,256]{1,0:T(8,128)S(1)}, u32[]{:S(2)}, u32[]{:S(2)}) collective-permute-start(f32[64,256]{1,0:T(8,128)S(1)} %fusion.10), channel_id=1, source_target_pairs={{0,6},{1,7},{2,0},{3,1},{4,2},{5,3},{6,4},{7,5},{16,22},{17,23},{1... | collective-permute-start | bytes 196616 | tf_op jit(solution)/shard_map/ppermute | solution.py:271
  81.8 38.8 %collective-permute-start.25 = (f32[2,256,256]{2,1,0:T(8,128)S(1)}, f32[2,256,256]{2,1,0:T(8,128)S(1)}, u32[]{:S(2)}, u32[]{:S(2)}) collective-permute-start(f32[2,256,256]{2,1,0:T(8,128)S(1)} %get-tuple-element.101), channel_id=1, source_target_pairs={{0,16},{16,32},{32,48},{48,64},{64,80},{80,96},{96,112},{112,0},{1... | collective-permute-start | bytes 1572872 | tf_op jit(solution)/shard_map/ppermute | solution.py:252
  88.5 33.0 %collective-permute-start.26 = (f32[2,256,256]{2,1,0:T(8,128)S(1)}, f32[2,256,256]{2,1,0:T(8,128)S(1)}, u32[]{:S(2)}, u32[]{:S(2)}) collective-permute-start(f32[2,256,256]{2,1,0:T(8,128)S(1)} %get-tuple-element.102), channel_id=1, source_target_pairs={{0,112},{16,0},{32,16},{48,32},{64,48},{80,64},{96,80},{112,96},{1... | collective-permute-start | bytes 1572872 | tf_op jit(solution)/shard_map/ppermute | solution.py:252
  110.3 15.8 %collective-permute-start.19 = (f32[64,256]{1,0:T(8,128)S(1)}, f32[64,256]{1,0:T(8,128)S(1)}, u32[]{:S(2)}, u32[]{:S(2)}) collective-permute-start(f32[64,256]{1,0:T(8,128)S(1)} %add_add_fusion.3), channel_id=1, source_target_pairs={{0,16},{1,17},{2,18},{3,19},{4,20},{5,21},{6,22},{7,23},{16,8},{17... | collective-permute-start | bytes 196616 | tf_op jit(solution)/shard_map/ppermute | solution.py:271
  111.9 15.1 %collective-permute-start.20 = (f32[64,256]{1,0:T(8,128)S(1)}, f32[64,256]{1,0:T(8,128)S(1)}, u32[]{:S(2)}, u32[]{:S(2)}) collective-permute-start(f32[64,256]{1,0:T(8,128)S(1)} %add_add_fusion.3), channel_id=1, source_target_pairs={{0,8},{1,9},{2,10},{3,11},{4,12},{5,13},{6,14},{7,15},{16,24},{17,... | collective-permute-start | bytes 196616 | tf_op jit(solution)/shard_map/ppermute | solution.py:271
  115.3 11.7 %collective-permute-start.21 = (f32[64,256]{1,0:T(8,128)S(1)}, f32[64,256]{1,0:T(8,128)S(1)}, u32[]{:S(2)}, u32[]{:S(2)}) collective-permute-start(f32[64,256]{1,0:T(8,128)S(1)} %add_add_fusion.3), channel_id=1, source_target_pairs={{0,24},{1,25},{2,26},{3,27},{4,28},{5,29},{6,30},{7,31},{16,0},{17... | collective-permute-start | bytes 196616 | tf_op jit(solution)/shard_map/ppermute | solution.py:271
  124.4 11.7 %collective-permute-start.27 = (f32[2,768,128]{2,1,0:T(8,128)}, f32[2,768,128]{2,1,0:T(8,128)}, u32[]{:S(2)}, u32[]{:S(2)}) collective-permute-start(f32[2,768,128]{2,1,0:T(8,128)} %get-tuple-element.100), channel_id=1, source_target_pairs={{0,1},{1,2},{2,3},{3,4},{4,5},{5,6},{6,7},{7,8},{8,9},{9,10},{10,1... | collective-permute-start | bytes 2359304 | tf_op jit(solution)/shard_map/ppermute | solution.py:252
  125.5 10.6 %collective-permute-start.28 = (f32[2,768,128]{2,1,0:T(8,128)}, f32[2,768,128]{2,1,0:T(8,128)}, u32[]{:S(2)}, u32[]{:S(2)}) collective-permute-start(f32[2,768,128]{2,1,0:T(8,128)} %get-tuple-element.99), channel_id=1, source_target_pairs={{0,15},{1,0},{2,1},{3,2},{4,3},{5,4},{6,5},{7,6},{8,7},{9,8},{10,9... | collective-permute-start | bytes 2359304 | tf_op jit(solution)/shard_map/ppermute | solution.py:252
  136.1 11.4 %collective-permute-start.29 = (f32[4,64,256]{2,1,0:T(8,128)S(1)}, f32[4,64,256]{2,1,0:T(8,128)}, u32[]{:S(2)}, u32[]{:S(2)}) collective-permute-start(f32[4,64,256]{2,1,0:T(8,128)S(1)} %bitcast_dynamic-update-slice_fusion.4), channel_id=1, source_target_pairs={{0,1},{1,0},{2,3},{3,2},{4,5},{5,4},{6,7},{7,6},{16,17},{17,16},{1... | collective-permute-start | bytes 786440 | tf_op jit(solution)/shard_map/ppermute | solution.py:271
  165.5 24.4 %collective-permute-start.34 = (f32[2,384,384]{2,1,0:T(8,128)S(1)}, f32[2,384,384]{2,1,0:T(8,128)S(1)}, u32[]{:S(2)}, u32[]{:S(2)}) collective-permute-start(f32[2,384,384]{2,1,0:T(8,128)S(1)} %get-tuple-element.67), channel_id=1, source_target_pairs={{0,15},{1,0},{2,1},{3,2},{4,3},{5,4},{6,5},{7,6},{8,7},{9,8},{10,9... | collective-permute-start | bytes 3538952 | tf_op jit(solution)/shard_map/ppermute | solution.py:252
  166.2 23.7 %collective-permute-start.35 = (f32[2,384,128]{2,1,0:T(8,128)S(1)}, f32[2,384,128]{2,1,0:T(8,128)S(1)}, u32[]{:S(2)}, u32[]{:S(2)}) collective-permute-start(f32[2,384,128]{2,1,0:T(8,128)S(1)} %get-tuple-element.68), channel_id=1, source_target_pairs={{0,112},{16,0},{32,16},{48,32},{64,48},{80,64},{96,80},{112,96},{1... | collective-permute-start | bytes 1179656 | tf_op jit(solution)/shard_map/ppermute | solution.py:252
  168.9 8.1 %collective-permute-start.32 = (f32[64,256]{1,0:T(8,128)S(1)}, f32[64,256]{1,0:T(8,128)S(1)}, u32[]{:S(2)}, u32[]{:S(2)}) collective-permute-start(f32[64,256]{1,0:T(8,128)S(1)} %get-tuple-element.114), channel_id=1, source_target_pairs={{0,64},{1,65},{2,66},{3,67},{4,68},{5,69},{6,70},{7,71},{16,80},{1... | collective-permute-start | bytes 196616 | tf_op jit(solution)/shard_map/ppermute | solution.py:271
  173.5 14.9 %collective-permute-start.33 = (f32[64,256]{1,0:T(8,128)S(1)}, f32[64,256]{1,0:T(8,128)S(1)}, u32[]{:S(2)}, u32[]{:S(2)}) collective-permute-start(f32[64,256]{1,0:T(8,128)S(1)} %get-tuple-element.113), channel_id=1, source_target_pairs={{0,96},{1,97},{2,98},{3,99},{4,100},{5,101},{6,102},{7,103},{16,11... | collective-permute-start | bytes 196616 | tf_op jit(solution)/shard_map/ppermute | solution.py:271
  190.0 11.8 %collective-permute-start.39 = (f32[2,384,128]{2,1,0:T(8,128)S(1)}, f32[2,384,128]{2,1,0:T(8,128)S(1)}, u32[]{:S(2)}, u32[]{:S(2)}) collective-permute-start(f32[2,384,128]{2,1,0:T(8,128)S(1)} %get-tuple-element.98), channel_id=1, source_target_pairs={{0,112},{16,0},{32,16},{48,32},{64,48},{80,64},{96,80},{112,96},{1... | collective-permute-start | bytes 1179656 | tf_op jit(solution)/shard_map/ppermute | solution.py:252
  192.2 17.8 %collective-permute-start.40 = (f32[2,384,128]{2,1,0:T(8,128)S(1)}, f32[2,384,128]{2,1,0:T(8,128)S(1)}, u32[]{:S(2)}, u32[]{:S(2)}) collective-permute-start(f32[2,384,128]{2,1,0:T(8,128)S(1)} %get-tuple-element.97), channel_id=1, source_target_pairs={{0,112},{16,0},{32,16},{48,32},{64,48},{80,64},{96,80},{112,96},{1... | collective-permute-start | bytes 1179656 | tf_op jit(solution)/shard_map/ppermute | solution.py:252
  210.1 7.2 %collective-permute-start.42 = (f32[64,256]{1,0:T(8,128)S(1)}, f32[64,256]{1,0:T(8,128)S(1)}, u32[]{:S(2)}, u32[]{:S(2)}) collective-permute-start(f32[64,256]{1,0:T(8,128)S(1)} %add_add_fusion.1), channel_id=1, source_target_pairs={{0,16},{1,17},{2,18},{3,19},{4,20},{5,21},{6,22},{7,23},{16,8},{17... | collective-permute-start | bytes 196616 | tf_op jit(solution)/shard_map/ppermute | solution.py:271
  210.1 7.2 %collective-permute-start.43 = (f32[64,256]{1,0:T(8,128)S(1)}, f32[64,256]{1,0:T(8,128)S(1)}, u32[]{:S(2)}, u32[]{:S(2)}) collective-permute-start(f32[64,256]{1,0:T(8,128)S(1)} %add_add_fusion.1), channel_id=1, source_target_pairs={{0,8},{1,9},{2,10},{3,11},{4,12},{5,13},{6,14},{7,15},{16,24},{17,... | collective-permute-start | bytes 196616 | tf_op jit(solution)/shard_map/ppermute | solution.py:271
  213.3 31.9 %collective-permute-start.48 = (f32[2,384,128]{2,1,0:T(8,128)S(1)}, f32[2,384,128]{2,1,0:T(8,128)S(1)}, u32[]{:S(2)}, u32[]{:S(2)}) collective-permute-start(f32[2,384,128]{2,1,0:T(8,128)S(1)} %get-tuple-element.103), channel_id=1, source_target_pairs={{0,112},{16,0},{32,16},{48,32},{64,48},{80,64},{96,80},{112,96},{1... | collective-permute-start | bytes 1179656 | tf_op jit(solution)/shard_map/ppermute | solution.py:252
  218.6 23.4 %collective-permute-start.45 = (f32[64,256]{1,0:T(8,128)S(1)}, f32[64,256]{1,0:T(8,128)S(1)}, u32[]{:S(2)}, u32[]{:S(2)}) collective-permute-start(f32[64,256]{1,0:T(8,128)S(1)} %get-tuple-element.81), channel_id=1, source_target_pairs={{0,32},{1,33},{2,34},{3,35},{4,36},{5,37},{6,38},{7,39},{16,48},{1... | collective-permute-start | bytes 196616 | tf_op jit(solution)/shard_map/ppermute | solution.py:271
  239.1 13.8 %collective-permute-start.41 = (f32[2,384,384]{2,1,0:T(8,128)S(1)}, f32[2,384,384]{2,1,0:T(8,128)S(1)}, u32[]{:S(2)}, u32[]{:S(2)}) collective-permute-start(f32[2,384,384]{2,1,0:T(8,128)S(1)} %get-tuple-element.73), channel_id=1, source_target_pairs={{0,15},{1,0},{2,1},{3,2},{4,3},{5,4},{6,5},{7,6},{8,7},{9,8},{10,9... | collective-permute-start | bytes 3538952 | tf_op jit(solution)/shard_map/ppermute | solution.py:252
  (36 other events, 339.1 us)
